TPU v7x, 32 devices: a whole 2x2x4 slice. The times are simulated.
32 devices in a mesh: groups: 2 (over y), row: 16 (over z, x, core).
Axes of the slice: x: 2, y: 2, z: 4, core: 2. Of those that a mesh axis runs over, the one named last changes fastest.
Arguments:
- spectra: bfloat16 [2, 2, 8192, 8192], P('groups', None, None, 'row'), parts along dimension 0, may hold values from -1.5 to 1.5
- pattern: int32 [64, 64], replicated, may hold values from 0 to 1, as said below
- counts: int32 [8192], replicated, may hold values from 1 to 8
Outputs:
- multiples: bfloat16 [2, 2, 8192, 8192], P('groups', None, 'row'), parts along dimension 0
There are 2 independent parts, one for each index of `groups`. A program takes and returns all parts, laid end to end along the dimension named above; an argument that names none is the same for every part. Nothing has to cross between parts.
Inputs may be any that keep to these rules, and one draw needn't show every extreme that they name: pattern[I, K] is 0 or 1, is 0 wherever |I - K| > 2, and is 1 on the diagonal.
All inputs are finite; a program needn't handle non-finite values.
Results may differ from a plain program's by a relative error of at most 0.0025.
Values may be sent and summed in bfloat16 or wider, within the bound.
A program may use at most 256 MiB of HBM per device.

v0:
```python
import jax
import jax.numpy as jnp
from jax import lax
from jax.sharding import PartitionSpec as P

TILE = 128
REACH = 2


def from_behind(value, axis, steps):
    count = lax.axis_size(axis)
    initial, last = (max(0, -steps), min(count, count - steps))
    return lax.ppermute(value, axis, [(source, source + steps) for source in range(initial, last)])


def per_device(spectra, pattern, counts):
    total = spectra.shape[2]
    rows_dev = spectra.shape[3]
    place = lax.axis_index("row")
    margin = REACH * TILE
    span = max(rows_dev, TILE) + 2 * margin
    tiles = total // TILE
    first_tile = place * rows_dev // TILE
    offset_rows = place * rows_dev - first_tile * TILE
    own_rows = lax.all_to_all(spectra, "row", split_axis=2, concat_axis=3, tiled=True)
    below = (margin + max(TILE - rows_dev, 0) + rows_dev - 1) // rows_dev
    above = (span - margin + rows_dev - 1) // rows_dev - 1
    pieces = []
    for offset in range(-below, above + 1):
        if offset == 0:
            pieces.append(own_rows)
        else:
            pieces.append(from_behind(own_rows, "row", -offset))
    joined = jnp.concatenate(pieces, axis=2)
    window = lax.dynamic_slice_in_dim(joined, below * rows_dev - margin - offset_rows, span, 2)
    tile_range = jnp.arange(tiles, dtype=jnp.int32)
    row_ids = place * rows_dev + jnp.arange(rows_dev, dtype=jnp.int32)
    inner_ids = (first_tile - REACH) * TILE + jnp.arange(span, dtype=jnp.int32)
    row_onehot = (row_ids[:, None] // TILE == tile_range[None, :]).astype(jnp.float32)
    inner_onehot = (inner_ids[:, None] // TILE == tile_range[None, :]).astype(jnp.float32)
    pattern_rows = jnp.dot(row_onehot, pattern.astype(jnp.float32), precision=lax.Precision.HIGHEST)
    aperture = jnp.dot(pattern_rows, inner_onehot.T, precision=lax.Precision.HIGHEST)
    padded_counts = jnp.pad(counts, (margin, margin), constant_values=1)
    weights = 1.0 / lax.dynamic_slice_in_dim(padded_counts, first_tile * TILE, span).astype(
        jnp.float32
    )
    factor = aperture * weights[None, :]
    wide_rows = jnp.pad(own_rows, ((0, 0), (0, 0), (0, 0), (margin, margin)))
    columns = lax.dynamic_slice_in_dim(wide_rows, first_tile * TILE, span, 3)
    left = (columns[0].astype(jnp.float32) * factor[None]).astype(jnp.bfloat16)
    stacked_left = jnp.concatenate(
        [jnp.concatenate([left[0], -left[1]], axis=1), jnp.concatenate([left[1], left[0]], axis=1)],
        axis=0,
    )
    product = jnp.dot(
        stacked_left, window[0].reshape(2 * span, total), preferred_element_type=jnp.float32
    )
    results = [product.astype(jnp.bfloat16).reshape(2, rows_dev, total)]
    return jnp.stack(results)


def solution(mesh):
    return jax.shard_map(
        per_device,
        mesh=mesh,
        in_specs=(P("groups", None, None, "row"), P(), P()),
        out_specs=P("groups", None, "row", None),
        check_vma=False,
    )
```

profile of v0, /device:TPU:17, one launch (start us, length us, event | category | flops | bytes accessed | tf_op | source)
XLA Modules:
  0.0 899.8 jit_solution(1148219069868233948)
XLA Ops:
  0.0 27.9 %copy.8 = bf16[1,2,8192,512]{3,1,0,2:T(2,128)(2,1)S(1)} copy(bf16[1,2,8192,512]{3,2,1,0:T(8,128)(2,1)} %param.3) | data formatting | bytes 33554432 | tf_op args[0]
  27.9 368.2 %all_to_all.18 = bf16[1,2,8192,512]{3,1,0,2:T(2,128)(2,1)S(1)} all-to-all(bf16[1,2,8192,512]{3,1,0,2:T(2,128)(2,1)S(1)} %copy.8), channel_id=1, replica_groups=mesh['groups'=2,'row'=16] {'row'}, dimensions={2} | all-to-all | bytes 33554432 | tf_op jit(solution)/shard_map/all_to_all | solution.py:25
  396.1 10.1 %copy.9 = bf16[1,2,8192,512]{3,2,1,0:T(8,128)(2,1)} copy(bf16[1,2,8192,512]{3,1,0,2:T(2,128)(2,1)S(1)} %all_to_all.18) | data formatting | bytes 33554432 | tf_op jit(solution)/shard_map/all_to_all | solution.py:25
  406.3 0.0 copy-start
  406.3 0.0 copy-start.1
  406.3 22.5 %copy.10 = bf16[1,2,512,16,512]{2,4,3,1,0:T(8,128)(2,1)} copy(bf16[1,2,512,16,512]{4,2,3,1,0:T(8,128)(2,1)} %bitcast.21) | data formatting | bytes 33554432 | tf_op jit(solution)/shard_map/all_to_all | solution.py:25
  428.8 2.4 collective-permute-start
  431.1 2.5 collective-permute-start.1
  433.7 0.0 copy-done
  433.7 0.1 fusion.16
  433.8 0.0 copy-done.1
  433.8 0.4 fusion.11
  434.2 2.6 convolution_multiply_fusion
  436.8 1.9 copy.11
  438.7 2.2 fusion.9
  440.9 0.1 fusion.23
  441.0 0.1 slice_bitcast_fusion
  441.1 350.3 %collective-permute-done = bf16[1,2,512,8192]{2,3,1,0:T(8,128)(2,1)} collective-permute-done((bf16[1,2,512,8192]{2,3,1,0:T(8,128)(2,1)}, bf16[1,2,512,8192]{2,3,1,0:T(8,128)(2,1)}, u32[]{:S(2)}, u32[]{:S(2)}) %collective-permute-start) | collective-permute-done | bytes 16777248 | tf_op jit(solution)/shard_map/ppermute | solution.py:13
  791.5 3.3 collective-permute-done.1
  794.8 23.4 %fusion.1 = bf16[1,2,1024,8192]{2,3,1,0:T(8,128)(2,1)} fusion(s32[]{:T(128)S(6)} %select_n.36, bf16[1,2,512,8192]{2,3,1,0:T(8,128)(2,1)} %collective-permute-done, bf16[1,2,512,8192]{2,3,1,0:T(8,128)(2,1)} %bitcast.20, bf16[1,2,512,8192]{2,3,1,0:T(8,128)(2,1)} %collective-permute-done.1), kind=kLoop, calls=%fused_computation.4 | loop fusion | flops 100663296 | bytes 83886080 | tf_op jit(solution)/shard_map/concatenate | solution.py:34
  818.2 40.5 %copy.12 = bf16[1,2,1024,8192]{3,2,1,0:T(8,128)(2,1)} copy(bf16[1,2,1024,8192]{2,3,1,0:T(8,128)(2,1)} %fusion.1) | data formatting | bytes 67108864 | tf_op jit(solution)/shard_map/dynamic_slice | solution.py:35
  858.7 41.2 %convolution_convert_fusion = bf16[1024,8192]{1,0:T(8,128)(2,1)} fusion(bf16[2048,8192]{1,0:T(8,128)(2,1)} %bitcast.22, bf16[512,1024]{0,1:T(8,128)(2,1)S(1)} %get-tuple-element.6, bf16[512,1024]{0,1:T(8,128)(2,1)S(1)} %get-tuple-element.5, bf16[512,1024]{0,1:T(8,128)(2,1)S(1)} %fusion.23), kind=kOutput, calls=%fused_computation.6 | convolution fusion | flops 34384904192 | bytes 53477376 | tf_op jit(solution)/shard_map/dot_general | solution.py:55
  (2 shorter events, 0.0 us)
Async XLA Ops:
  406.3 27.4 %copy-start = (s32[8192]{0:T(1024)S(1)}, s32[8192]{0:T(1024)}, u32[]{:S(2)}) copy-start(s32[8192]{0:T(1024)} %param.5) | copy-start | bytes 98308
  406.3 27.5 %copy-start.1 = (s32[64,64]{1,0:T(8,128)S(1)}, s32[64,64]{1,0:T(8,128)}, u32[]{:S(2)}) copy-start(s32[64,64]{1,0:T(8,128)} %param.4) | copy-start | bytes 49156
  428.8 362.7 %collective-permute-start = (bf16[1,2,512,8192]{2,3,1,0:T(8,128)(2,1)}, bf16[1,2,512,8192]{2,3,1,0:T(8,128)(2,1)}, u32[]{:S(2)}, u32[]{:S(2)}) collective-permute-start(bf16[1,2,512,8192]{2,3,1,0:T(8,128)(2,1)} %bitcast.17), channel_id=1, source_target_pairs={{0,1},{1,2},{2,3},{3,4},{4,5},{5,6},{6,7},{7,8},{8,9},{9,10},{10,1... | collective-permute-start | bytes 50331656 | tf_op jit(solution)/shard_map/ppermute | solution.py:13
  431.1 363.6 %collective-permute-start.1 = (bf16[1,2,512,8192]{2,3,1,0:T(8,128)(2,1)}, bf16[1,2,512,8192]{2,3,1,0:T(8,128)(2,1)}, u32[]{:S(2)}, u32[]{:S(2)}) collective-permute-start(bf16[1,2,512,8192]{2,3,1,0:T(8,128)(2,1)} %bitcast.18), channel_id=1, source_target_pairs={{1,0},{2,1},{3,2},{4,3},{5,4},{6,5},{7,6},{8,7},{9,8},{10,9},{11,1... | collective-permute-start | bytes 50331656 | tf_op jit(solution)/shard_map/ppermute | solution.py:13
where the time goes:
time: 902 us; the launch traced here: 900 us
  blocking collectives  368 us (41%)
  waiting for transfers between devices  354 us (39%)
  local copies, waits for them, and re-layouts  103 us (11%)
  matrix products  44.1 us (5%)
  other arithmetic  25.8 us (3%)
    all_to_all x1, blocking collectives, per_device(): lax.all_to_all(spectra, 'row', split_axis=2, concat_axis=3, tiled=True)  368 us
    ppermute x2, waiting for transfers between devices, from_behind(): lax.ppermute(value, axis, [(source, source + steps) for source in range(i...  354 us
    dot_general x1, matrix products, per_device(): jnp.dot(stacked_left, window[0].reshape(2 * span, total), preferred_eleme...  41.2 us
    dynamic_slice x1, local copies, waits for them, and re-layouts, per_device(): lax.dynamic_slice_in_dim(joined, below * rows_dev - margin - offset_rows,...  40.5 us
    all_to_all x2, local copies, waits for them, and re-layouts, per_device(): lax.all_to_all(spectra, 'row', split_axis=2, concat_axis=3, tiled=True)  32.6 us
    unnamed x5, local copies, waits for them, and re-layouts  27.9 us
    concatenate x1, other arithmetic, per_device(): joined = jnp.concatenate(pieces, axis=2)  23.4 us
  transfers between devices with their start and end apart: 2, of which 2 were waited for; matrix products, arithmetic and copies ran while one was open for 1% of the time, Pallas kernels for 0%

commit v1 on v0

--- a/solution.py
+++ b/solution.py
@@ -1,10 +1,18 @@
+import functools
+
 import jax
 import jax.numpy as jnp
 from jax import lax
+from jax.experimental import pallas as pl
+from jax.experimental.pallas import tpu as pltpu
 from jax.sharding import PartitionSpec as P
 
 TILE = 128
 REACH = 2
+WIDE = 2 * REACH + 1
+CORES = 4
+AHEAD = 2
+VMEM_BYTES = 62 * 2**20
 
 
 def from_behind(value, axis, steps):
@@ -13,7 +21,7 @@
     return lax.ppermute(value, axis, [(source, source + steps) for source in range(initial, last)])
 
 
-def per_device(spectra, pattern, counts):
+def by_rows(spectra, pattern, counts):
     total = spectra.shape[2]
     rows_dev = spectra.shape[3]
     place = lax.axis_index("row")
@@ -59,6 +67,315 @@
     return jnp.stack(results)
 
 
+def window_start(tile, tiles):
+    return jnp.clip(tile - REACH, 0, tiles - WIDE)
+
+
+def plane_kernel(planes, src, pat, weights, out, held, band, left, done,
+                 band_send, band_recv, edge_send, edge_recv,
+                 part_send, part_recv, out_send, out_recv):
+    tiles = src.shape[1]
+    cols = src.shape[3]
+    own_tiles = cols // TILE
+    plane_tiles = CORES * own_tiles
+    me = lax.axis_index("row")
+    plane = me // CORES
+    m = me % CORES
+    core_mate = me + 1 - 2 * (me % 2)
+    x_mate = plane * CORES + (m + 2) % CORES
+    first = plane * plane_tiles
+    low_first = m >= 2
+
+    def device(index):
+        return dict(device_id={"row": index}, device_id_type=pl.DeviceIdType.MESH)
+
+    barrier = pltpu.get_barrier_semaphore()
+    count = planes * CORES
+
+    def greet(step, carry):
+        pl.semaphore_signal(barrier, inc=1, **device(lax.rem(me + step, count)))
+        return carry
+
+    lax.fori_loop(1, count, greet, 0)
+    pl.semaphore_wait(barrier, count - 1)
+
+    def band_view(u):
+        tile = me * own_tiles + u
+        return src.at[:, pl.ds(window_start(tile, tiles), WIDE), :, pl.ds(u * TILE, TILE)]
+
+    def band_slot(member, u):
+        return band.at[member * own_tiles + u + REACH]
+
+    def band_copy(kind, member, u, target):
+        source = band_slot(member, u) if kind == 2 else band_view(u)
+        return pltpu.make_async_remote_copy(
+            src_ref=source, dst_ref=band_slot(member, u),
+            send_sem=band_send.at[kind, u], recv_sem=band_recv.at[kind, u], **device(target))
+
+    def band_local(u):
+        return pltpu.make_async_copy(band_view(u), band_slot(m, u), band_recv.at[3, u])
+
+    for u in range(own_tiles):
+        band_copy(1, m, u, x_mate).start()
+    for u in range(own_tiles):
+        band_local(u).start()
+        band_copy(0, m, u, core_mate).start()
+
+    def edge_copy(side, u, dest):
+        if side == 0:
+            column = own_tiles - REACH + u
+            row, slot, place = me * own_tiles + column + 1, u, WIDE - REACH
+        else:
+            column = u
+            row, slot, place = me * own_tiles + column - REACH, plane_tiles + REACH + u, 0
+        row = jnp.clip(row, 0, tiles - REACH)
+        return pltpu.make_async_remote_copy(
+            src_ref=src.at[:, pl.ds(row, REACH), :, pl.ds(column * TILE, TILE)],
+            dst_ref=band.at[slot, :, pl.ds(place, REACH)],
+            send_sem=edge_send.at[side, u, dest % CORES], recv_sem=edge_recv.at[side, u],
+            **device(dest))
+
+    sends_low = jnp.logical_and(m == CORES - 1, plane < planes - 1)
+    sends_high = jnp.logical_and(m == 0, plane > 0)
+
+    @pl.when(sends_low)
+    def _():
+        for u in range(REACH):
+            for mate in range(CORES):
+                edge_copy(0, u, (plane + 1) * CORES + mate).start()
+
+    @pl.when(sends_high)
+    def _():
+        for u in range(REACH):
+            for mate in range(CORES):
+                edge_copy(1, u, (plane - 1) * CORES + mate).start()
+
+    def parts(step, to_plane, from_plane, act, local=False):
+        base = to_plane * plane_tiles
+
+        def piece(start, size, c, slot):
+            source = src.at[c, pl.ds(base - REACH + start, size)]
+            dest = held.at[from_plane, pl.ds(start, size), c]
+            if local:
+                return pltpu.make_async_copy(source, dest, part_recv.at[from_plane, slot, c])
+            return pltpu.make_async_remote_copy(
+                src_ref=source, dst_ref=dest,
+                send_sem=part_send.at[to_plane, slot, c],
+                recv_sem=part_recv.at[from_plane, slot, c],
+                **device(to_plane * CORES + m))
+
+        slot = jnp.where(low_first, step, CORES + 1 - step)
+
+        def both(start, size):
+            for c in range(2):
+                act(piece(start, size, c, slot))
+
+        if 1 <= step <= CORES:
+            both(REACH + (slot - 1) * own_tiles, own_tiles)
+        else:
+            @pl.when(jnp.logical_and(slot == 0, to_plane > 0))
+            def _():
+                both(0, REACH)
+
+            @pl.when(jnp.logical_and(slot == CORES + 1, to_plane < planes - 1))
+            def _():
+                both(REACH + plane_tiles, REACH)
+
+    def start(copy):
+        copy.start()
+
+    steps = CORES + 2
+    offsets = [o for k in range(1, planes // 2 + 1) for o in dict.fromkeys((k, planes - k))]
+
+    def send_step(step):
+        for o in offsets:
+            parts(step, lax.rem(plane + o, planes), plane, start)
+
+    for step in range(steps):
+        parts(step, plane, plane, start, local=True)
+    for step in range(AHEAD):
+        send_step(step)
+
+    for u in range(own_tiles):
+        band_copy(1, (m + 2) % CORES, u, x_mate).wait_recv()
+        band_copy(2, (m + 2) % CORES, u, core_mate).start()
+    core_m = core_mate % CORES
+    for u in range(own_tiles):
+        band_local(u).wait()
+        band_copy(0, core_m, u, core_mate).wait_recv()
+        band_copy(2, (core_m + 2) % CORES, u, core_mate).wait_recv()
+
+    @pl.when(plane > 0)
+    def _():
+        for u in range(REACH):
+            edge_copy(0, u, me).wait_recv()
+
+    @pl.when(plane < planes - 1)
+    def _():
+        for u in range(REACH):
+            edge_copy(1, u, me).wait_recv()
+
+    def build(index, carry):
+        i, t = index // WIDE, index % WIDE
+        tile = first + i
+        inner = window_start(tile, tiles) + t
+        j = jnp.clip(tile - window_start(inner, tiles), 0, WIDE - 1)
+        slot = inner - first + REACH
+        factor = pat[tile, inner].astype(jnp.float32) * weights[pl.ds(inner, 1), :]
+        re = (band[slot, 0, j].astype(jnp.float32) * factor).astype(jnp.bfloat16)
+        im = (band[slot, 1, j].astype(jnp.float32) * factor).astype(jnp.bfloat16)
+        left[i, t, 0:TILE, 0:TILE] = re
+        left[i, t, 0:TILE, TILE:2 * TILE] = -im
+        left[i, t, TILE:2 * TILE, 0:TILE] = im
+        left[i, t, TILE:2 * TILE, TILE:2 * TILE] = re
+        return carry
+
+    lax.fori_loop(0, plane_tiles * WIDE, build, 0)
+
+    def out_copy(from_plane, group, sender, local=False):
+        dest = out.at[:, :, pl.ds(pl.multiple_of((from_plane * CORES + sender) * cols, cols), cols)]
+        source = done.at[from_plane, group]
+        if local:
+            return pltpu.make_async_copy(source, dest, out_send.at[from_plane, group])
+        return pltpu.make_async_remote_copy(
+            src_ref=source, dst_ref=dest,
+            send_sem=out_send.at[from_plane, group], recv_sem=out_recv.at[from_plane, sender],
+            **device(plane * CORES + group))
+
+    def multiply(order, from_plane):
+        group = jnp.where(low_first, order, CORES - 1 - order)
+
+        def one(r, carry):
+            i = group * own_tiles + r
+            begin = window_start(first + i, tiles) - first + REACH
+            total = None
+            for t in range(WIDE):
+                term = jnp.dot(left[i, t], held[from_plane, begin + t].reshape(2 * TILE, cols),
+                               preferred_element_type=jnp.float32)
+                total = term if total is None else total + term
+            rows = pl.ds(pl.multiple_of(r * TILE, TILE), TILE)
+            done[from_plane, group, 0, rows, :] = total[:TILE].astype(jnp.bfloat16)
+            done[from_plane, group, 1, rows, :] = total[TILE:].astype(jnp.bfloat16)
+            return carry
+
+        lax.fori_loop(0, own_tiles, one, 0)
+
+        @pl.when(group == m)
+        def _():
+            out_copy(from_plane, group, m, local=True).start()
+
+        @pl.when(group != m)
+        def _():
+            out_copy(from_plane, group, m).start()
+
+    for step in range(steps):
+        parts(step, plane, plane, lambda copy: copy.wait(), local=True)
+
+    def own(order, carry):
+        multiply(order, plane)
+        return carry
+
+    lax.fori_loop(0, CORES, own, 0)
+
+    for step in range(steps):
+        if step and step + AHEAD - 1 < steps:
+            send_step(step + AHEAD - 1)
+        for o in offsets:
+            sender = lax.rem(plane + planes - o, planes)
+            parts(step, plane, sender, lambda copy: copy.wait_recv())
+            if step >= 2:
+                multiply(step - 2, sender)
+
+    for u in range(own_tiles):
+        for kind in range(3):
+            band_copy(kind, m, u, core_mate).wait_send()
+
+    @pl.when(sends_low)
+    def _():
+        for u in range(REACH):
+            for mate in range(CORES):
+                edge_copy(0, u, (plane + 1) * CORES + mate).wait_send()
+
+    @pl.when(sends_high)
+    def _():
+        for u in range(REACH):
+            for mate in range(CORES):
+                edge_copy(1, u, (plane - 1) * CORES + mate).wait_send()
+
+    for step in range(steps):
+        for o in offsets:
+            parts(step, lax.rem(plane + o, planes), plane, lambda copy: copy.wait_send())
+
+    def finish(index, carry):
+        from_plane, group = index // CORES, index % CORES
+
+        @pl.when(group == m)
+        def _():
+            out_copy(from_plane, group, m, local=True).wait()
+
+        @pl.when(group != m)
+        def _():
+            out_copy(from_plane, group, m).wait_send()
+            out_copy(from_plane, group, group).wait_recv()
+
+        return carry
+
+    lax.fori_loop(0, planes * CORES, finish, 0)
+
+
+def by_planes(spectra, pattern, counts):
+    _, parts, total, cols = spectra.shape
+    devices = lax.axis_size("row")
+    planes = devices // CORES
+    tiles = total // TILE
+    own_tiles = cols // TILE
+    plane_tiles = CORES * own_tiles
+    reach_tiles = plane_tiles + 2 * REACH
+    weights = (1.0 / counts.astype(jnp.float32)).reshape(tiles, TILE)
+    dma = pltpu.SemaphoreType.DMA
+    product = pl.pallas_call(
+        functools.partial(plane_kernel, planes),
+        out_shape=jax.ShapeDtypeStruct((parts, cols, total), jnp.bfloat16),
+        in_specs=[
+            pl.BlockSpec(memory_space=pl.ANY),
+            pl.BlockSpec(memory_space=pltpu.SMEM),
+            pl.BlockSpec(memory_space=pltpu.VMEM),
+        ],
+        out_specs=pl.BlockSpec(memory_space=pl.ANY),
+        scratch_shapes=[
+            pltpu.VMEM((planes, reach_tiles, 2, TILE, cols), jnp.bfloat16),
+            pltpu.VMEM((reach_tiles, 2, WIDE, TILE, TILE), jnp.bfloat16),
+            pltpu.VMEM((plane_tiles, WIDE, 2 * TILE, 2 * TILE), jnp.bfloat16),
+            pltpu.VMEM((planes, CORES, 2, cols, cols), jnp.bfloat16),
+            dma((3, own_tiles)),
+            dma((4, own_tiles)),
+            dma((2, REACH, CORES)),
+            dma((2, REACH)),
+            dma((planes, CORES + 2, 2)),
+            dma((planes, CORES + 2, 2)),
+            dma((planes, CORES)),
+            dma((planes, CORES)),
+        ],
+        compiler_params=pltpu.CompilerParams(
+            collective_id=0, has_side_effects=True, vmem_limit_bytes=VMEM_BYTES),
+        cost_estimate=pl.CostEstimate(
+            flops=4 * total * parts * cols * WIDE * TILE, bytes_accessed=2 * spectra.nbytes, transcendentals=0),
+    )(spectra.reshape(parts, tiles, TILE, cols), pattern, weights)
+    return product[None]
+
+
+def fits(spectra):
+    devices = lax.axis_size("row")
+    cols = spectra.shape[3]
+    return devices % CORES == 0 and devices > CORES and cols % (2 * TILE) == 0 and spectra.shape[0] == 1
+
+
+def per_device(spectra, pattern, counts):
+    if fits(spectra):
+        return by_planes(spectra, pattern, counts)
+    return by_rows(spectra, pattern, counts)
+
+
 def solution(mesh):
     return jax.shard_map(
         per_device,

time: 902 us -> 468 us (0.52)
  the two profiles are of different devices: /device:TPU:17 before, /device:TPU:19 now
where the time goes in v1:
time: 468 us
  Pallas kernels  453 us (97%)
  local copies, waits for them, and re-layouts  14 us (3%)
    pallas_call x1, Pallas kernels, by_planes(): pl.pallas_call(functools.partial(plane_kernel, planes), out_shape=jax.Sha...  453 us
    unnamed x1, local copies, waits for them, and re-layouts  14 us

profile of v1, /device:TPU:19, one launch (start us, length us, event | category | flops | bytes accessed | tf_op | source)
XLA Modules:
  0.0 468.1 jit_solution(12233119259091822150)
XLA Ops:
  0.0 1.4 divide_bitcast_fusion.weights
  1.4 452.8 %shard_map.37 = bf16[2,512,8192]{2,1,0:T(8,128)(2,1)} custom-call(bf16[2,64,128,512]{3,2,1,0:T(8,128)(2,1)} %bitcast.5, s32[64,64]{1,0:T(8,128)} %pat.1, f32[64,128]{1,0:T(8,128)} %divide_bitcast_fusion.weights), custom_call_target="tpu_custom_call" | custom-call | flops 21474836480 | bytes 33554432 | tf_op jit(solution)/shard_map/pallas_call | solution.py:336
  454.2 14.0 %copy.5 = bf16[1,2,512,8192]{3,2,1,0:T(8,128)(2,1)} copy(bf16[1,2,512,8192]{3,2,1,0:T(8,128)(2,1)} %bitcast.4) | data formatting | bytes 33554432

commit v2 on v1

--- a/solution.py
+++ b/solution.py
@@ -11,7 +11,7 @@
 REACH = 2
 WIDE = 2 * REACH + 1
 CORES = 4
-AHEAD = 2
+AHEAD = 4
 VMEM_BYTES = 62 * 2**20
 
 
@@ -73,7 +73,7 @@
 
 def plane_kernel(planes, src, pat, weights, out, held, band, left, done,
                  band_send, band_recv, edge_send, edge_recv,
-                 part_send, part_recv, out_send, out_recv):
+                 part_send, part_recv, pass_send, out_send, out_recv):
     tiles = src.shape[1]
     cols = src.shape[3]
     own_tiles = cols // TILE
@@ -85,6 +85,8 @@
     x_mate = plane * CORES + (m + 2) % CORES
     first = plane * plane_tiles
     low_first = m >= 2
+    odd = plane % 2
+    far_planes = [2 - 2 * (plane // 2) + k for k in range(2)]
 
     def device(index):
         return dict(device_id={"row": index}, device_id_type=pl.DeviceIdType.MESH)
@@ -121,7 +123,7 @@
         band_local(u).start()
         band_copy(0, m, u, core_mate).start()
 
-    def edge_copy(side, u, dest):
+    def edge_copy(side, u, dest, relay=0):
         if side == 0:
             column = own_tiles - REACH + u
             row, slot, place = me * own_tiles + column + 1, u, WIDE - REACH
@@ -129,10 +131,11 @@
             column = u
             row, slot, place = me * own_tiles + column - REACH, plane_tiles + REACH + u, 0
         row = jnp.clip(row, 0, tiles - REACH)
+        landing = band.at[slot, :, pl.ds(place, REACH)]
+        source = landing if relay else src.at[:, pl.ds(row, REACH), :, pl.ds(column * TILE, TILE)]
         return pltpu.make_async_remote_copy(
-            src_ref=src.at[:, pl.ds(row, REACH), :, pl.ds(column * TILE, TILE)],
-            dst_ref=band.at[slot, :, pl.ds(place, REACH)],
-            send_sem=edge_send.at[side, u, dest % CORES], recv_sem=edge_recv.at[side, u],
+            src_ref=source, dst_ref=landing,
+            send_sem=edge_send.at[side, u, relay], recv_sem=edge_recv.at[side, u],
             **device(dest))
 
     sends_low = jnp.logical_and(m == CORES - 1, plane < planes - 1)
@@ -141,58 +144,86 @@
     @pl.when(sends_low)
     def _():
         for u in range(REACH):
-            for mate in range(CORES):
-                edge_copy(0, u, (plane + 1) * CORES + mate).start()
+            edge_copy(0, u, (plane + 1) * CORES + m).start()
 
     @pl.when(sends_high)
     def _():
         for u in range(REACH):
-            for mate in range(CORES):
-                edge_copy(1, u, (plane - 1) * CORES + mate).start()
-
-    def parts(step, to_plane, from_plane, act, local=False):
-        base = to_plane * plane_tiles
-
-        def piece(start, size, c, slot):
-            source = src.at[c, pl.ds(base - REACH + start, size)]
-            dest = held.at[from_plane, pl.ds(start, size), c]
-            if local:
-                return pltpu.make_async_copy(source, dest, part_recv.at[from_plane, slot, c])
-            return pltpu.make_async_remote_copy(
-                src_ref=source, dst_ref=dest,
-                send_sem=part_send.at[to_plane, slot, c],
-                recv_sem=part_recv.at[from_plane, slot, c],
-                **device(to_plane * CORES + m))
-
-        slot = jnp.where(low_first, step, CORES + 1 - step)
-
-        def both(start, size):
-            for c in range(2):
-                act(piece(start, size, c, slot))
-
-        if 1 <= step <= CORES:
-            both(REACH + (slot - 1) * own_tiles, own_tiles)
+            edge_copy(1, u, (plane - 1) * CORES + m).start()
+
+    units = plane_tiles // REACH + 2
+
+    def unit_copy(unit, to_plane, from_plane):
+        start = unit * REACH
+        return pltpu.make_async_remote_copy(
+            src_ref=src.at[:, pl.ds(to_plane * plane_tiles - REACH + start, REACH)],
+            dst_ref=held.at[from_plane, :, pl.ds(start, REACH)],
+            send_sem=part_send.at[to_plane, unit], recv_sem=part_recv.at[from_plane, unit],
+            **device(to_plane * CORES + m))
+
+    def parts(step, to_plane, from_plane, receiving, act):
+        low_edge = to_plane % 2 == 1
+        shared = jnp.where(low_edge, 1, units - 2)
+        far = to_plane // 2 != from_plane // 2
+
+        def one_end(unit):
+            exists = jnp.where(unit == 0, to_plane > 0, to_plane < planes - 1)
+            passed_on = jnp.logical_and(far, jnp.where(low_edge, unit == 0, unit == units - 1))
+            if not receiving:
+                exists = jnp.logical_and(exists, jnp.logical_not(passed_on))
+
+            @pl.when(exists)
+            def _():
+                act(unit_copy(unit, to_plane, from_plane))
+
+        if step == 0:
+            act(unit_copy(shared, to_plane, from_plane))
+        elif step == 1:
+            one_end(jnp.where(low_first, 0, units - 1))
+        elif step == units - 1:
+            one_end(jnp.where(low_first, units - 1, 0))
         else:
-            @pl.when(jnp.logical_and(slot == 0, to_plane > 0))
-            def _():
-                both(0, REACH)
-
-            @pl.when(jnp.logical_and(slot == CORES + 1, to_plane < planes - 1))
-            def _():
-                both(REACH + plane_tiles, REACH)
+            j = step - 2
+            act(unit_copy(jnp.where(low_first, jnp.where(low_edge, 2 + j, 1 + j),
+                                    jnp.where(low_edge, units - 2 - j, units - 3 - j)),
+                          to_plane, from_plane))
+
+    def pass_on(from_plane, act):
+        mine = jnp.where(odd == 1, 1, units - 2)
+        theirs = jnp.where(odd == 1, units - 1, 0)
+        act(pltpu.make_async_remote_copy(
+            src_ref=held.at[from_plane, :, pl.ds(mine * REACH, REACH)],
+            dst_ref=held.at[from_plane, :, pl.ds(theirs * REACH, REACH)],
+            send_sem=pass_send.at[from_plane], recv_sem=part_recv.at[from_plane, theirs],
+            **device((plane + 1 - 2 * odd) * CORES + m)))
+
+    def own_columns(act):
+        def piece(start, size, k):
+            act(pltpu.make_async_copy(
+                src.at[:, pl.ds(first - REACH + start, size)],
+                held.at[plane, :, pl.ds(start, size)], part_recv.at[plane, k]))
+
+        piece(REACH, plane_tiles, 1)
+
+        @pl.when(plane > 0)
+        def _():
+            piece(0, REACH, 0)
+
+        @pl.when(plane < planes - 1)
+        def _():
+            piece(REACH + plane_tiles, REACH, units - 1)
 
     def start(copy):
         copy.start()
 
-    steps = CORES + 2
+    steps = units
     offsets = [o for k in range(1, planes // 2 + 1) for o in dict.fromkeys((k, planes - k))]
 
     def send_step(step):
         for o in offsets:
-            parts(step, lax.rem(plane + o, planes), plane, start)
-
-    for step in range(steps):
-        parts(step, plane, plane, start, local=True)
+            parts(step, lax.rem(plane + o, planes), plane, False, start)
+
+    own_columns(start)
     for step in range(AHEAD):
         send_step(step)
 
@@ -205,15 +236,23 @@
         band_copy(0, core_m, u, core_mate).wait_recv()
         band_copy(2, (core_m + 2) % CORES, u, core_mate).wait_recv()
 
-    @pl.when(plane > 0)
-    def _():
+    relays_low = jnp.logical_and(m == CORES - 1, plane > 0)
+    relays_high = jnp.logical_and(m == 0, plane < planes - 1)
+
+    def edge_relay(side, act):
         for u in range(REACH):
-            edge_copy(0, u, me).wait_recv()
-
-    @pl.when(plane < planes - 1)
-    def _():
-        for u in range(REACH):
-            edge_copy(1, u, me).wait_recv()
+            for hop in range(1, CORES):
+                act(edge_copy(side, u, plane * CORES + (m + hop) % CORES, hop))
+
+    for side, present, relays in ((0, plane > 0, relays_low), (1, plane < planes - 1, relays_high)):
+        @pl.when(present)
+        def _(side=side):
+            for u in range(REACH):
+                edge_copy(side, u, me).wait_recv()
+
+        @pl.when(relays)
+        def _(side=side):
+            edge_relay(side, lambda copy: copy.start())
 
     def build(index, carry):
         i, t = index // WIDE, index % WIDE
@@ -250,8 +289,8 @@
             begin = window_start(first + i, tiles) - first + REACH
             total = None
             for t in range(WIDE):
-                term = jnp.dot(left[i, t], held[from_plane, begin + t].reshape(2 * TILE, cols),
-                               preferred_element_type=jnp.float32)
+                right = jnp.concatenate([held[from_plane, c, begin + t] for c in range(2)], axis=0)
+                term = jnp.dot(left[i, t], right, preferred_element_type=jnp.float32)
                 total = term if total is None else total + term
             rows = pl.ds(pl.multiple_of(r * TILE, TILE), TILE)
             done[from_plane, group, 0, rows, :] = total[:TILE].astype(jnp.bfloat16)
@@ -268,8 +307,7 @@
         def _():
             out_copy(from_plane, group, m).start()
 
-    for step in range(steps):
-        parts(step, plane, plane, lambda copy: copy.wait(), local=True)
+    own_columns(lambda copy: copy.wait())
 
     def own(order, carry):
         multiply(order, plane)
@@ -277,14 +315,19 @@
 
     lax.fori_loop(0, CORES, own, 0)
 
+    ready = [steps - 1 if g == CORES - 1 else 2 * g + 4 for g in range(CORES)]
     for step in range(steps):
         if step and step + AHEAD - 1 < steps:
             send_step(step + AHEAD - 1)
         for o in offsets:
             sender = lax.rem(plane + planes - o, planes)
-            parts(step, plane, sender, lambda copy: copy.wait_recv())
-            if step >= 2:
-                multiply(step - 2, sender)
+            parts(step, plane, sender, True, lambda copy: copy.wait_recv())
+            if step == 0:
+                @pl.when(sender // 2 != plane // 2)
+                def _():
+                    pass_on(sender, start)
+            elif step in ready:
+                multiply(ready.index(step), sender)
 
     for u in range(own_tiles):
         for kind in range(3):
@@ -293,18 +336,23 @@
     @pl.when(sends_low)
     def _():
         for u in range(REACH):
-            for mate in range(CORES):
-                edge_copy(0, u, (plane + 1) * CORES + mate).wait_send()
+            edge_copy(0, u, (plane + 1) * CORES + m).wait_send()
 
     @pl.when(sends_high)
     def _():
         for u in range(REACH):
-            for mate in range(CORES):
-                edge_copy(1, u, (plane - 1) * CORES + mate).wait_send()
-
+            edge_copy(1, u, (plane - 1) * CORES + m).wait_send()
+
+    for side, relays in ((0, relays_low), (1, relays_high)):
+        @pl.when(relays)
+        def _(side=side):
+            edge_relay(side, lambda copy: copy.wait_send())
+
+    for k in range(2):
+        pass_on(far_planes[k], lambda copy: copy.wait_send())
     for step in range(steps):
         for o in offsets:
-            parts(step, lax.rem(plane + o, planes), plane, lambda copy: copy.wait_send())
+            parts(step, lax.rem(plane + o, planes), plane, False, lambda copy: copy.wait_send())
 
     def finish(index, carry):
         from_plane, group = index // CORES, index % CORES
@@ -331,6 +379,7 @@
     own_tiles = cols // TILE
     plane_tiles = CORES * own_tiles
     reach_tiles = plane_tiles + 2 * REACH
+    units = reach_tiles // REACH
     weights = (1.0 / counts.astype(jnp.float32)).reshape(tiles, TILE)
     dma = pltpu.SemaphoreType.DMA
     product = pl.pallas_call(
@@ -343,7 +392,7 @@
         ],
         out_specs=pl.BlockSpec(memory_space=pl.ANY),
         scratch_shapes=[
-            pltpu.VMEM((planes, reach_tiles, 2, TILE, cols), jnp.bfloat16),
+            pltpu.VMEM((planes, 2, reach_tiles, TILE, cols), jnp.bfloat16),
             pltpu.VMEM((reach_tiles, 2, WIDE, TILE, TILE), jnp.bfloat16),
             pltpu.VMEM((plane_tiles, WIDE, 2 * TILE, 2 * TILE), jnp.bfloat16),
             pltpu.VMEM((planes, CORES, 2, cols, cols), jnp.bfloat16),
@@ -351,8 +400,9 @@
             dma((4, own_tiles)),
             dma((2, REACH, CORES)),
             dma((2, REACH)),
-            dma((planes, CORES + 2, 2)),
-            dma((planes, CORES + 2, 2)),
+            dma((planes, units)),
+            dma((planes, units)),
+            dma((planes,)),
             dma((planes, CORES)),
             dma((planes, CORES)),
         ],
@@ -367,7 +417,7 @@
 def fits(spectra):
     devices = lax.axis_size("row")
     cols = spectra.shape[3]
-    return devices % CORES == 0 and devices > CORES and cols % (2 * TILE) == 0 and spectra.shape[0] == 1
+    return devices == 4 * CORES and cols == 2 * REACH * TILE and spectra.shape[0] == 1
 
 
 def per_device(spectra, pattern, counts):

time: 468 us -> 422 us (0.902)
  Pallas kernels: 453 us -> 404 us
    pallas_call x1, Pallas kernels: 453 us -> 404 us  [by_planes(): pl.pallas_call(functools.partial(plane_kernel, planes), out_shape=jax.Sha...]
where the time goes in v2:
time: 422 us; the launch traced here: 420 us
  Pallas kernels  404 us (96%)
  local copies, waits for them, and re-layouts  14 us (3%)
    pallas_call x1, Pallas kernels, by_planes(): pl.pallas_call(functools.partial(plane_kernel, planes), out_shape=jax.Sha...  404 us
    unnamed x1, local copies, waits for them, and re-layouts  14 us

profile of v2, /device:TPU:19, one launch (start us, length us, event | category | flops | bytes accessed | tf_op | source)
XLA Modules:
  0.0 419.8 jit_solution(8384511259404577911)
XLA Ops:
  0.0 1.4 divide_bitcast_fusion.weights
  1.4 404.5 %shard_map.37 = bf16[2,512,8192]{2,1,0:T(8,128)(2,1)} custom-call(bf16[2,64,128,512]{3,2,1,0:T(8,128)(2,1)} %bitcast.5, s32[64,64]{1,0:T(8,128)} %pat.1, f32[64,128]{1,0:T(8,128)} %divide_bitcast_fusion.weights), custom_call_target="tpu_custom_call" | custom-call | flops 21474836480 | bytes 33554432 | tf_op jit(solution)/shard_map/pallas_call | solution.py:385
  405.9 14.0 %copy.5 = bf16[1,2,512,8192]{3,2,1,0:T(8,128)(2,1)} copy(bf16[1,2,512,8192]{3,2,1,0:T(8,128)(2,1)} %bitcast.4) | data formatting | bytes 33554432

commit v3 on v2

--- a/solution.py
+++ b/solution.py
@@ -217,7 +217,7 @@
         copy.start()
 
     steps = units
-    offsets = [o for k in range(1, planes // 2 + 1) for o in dict.fromkeys((k, planes - k))]
+    offsets = [o for k in range(planes // 2, 0, -1) for o in dict.fromkeys((k, planes - k))]
 
     def send_step(step):
         for o in offsets:

time: 422 us -> 422 us (level)
  no operation moved by 1% of the time
where the time goes in v3:
time: 422 us; the launch traced here: 419 us
  Pallas kernels  403 us (95%)
  local copies, waits for them, and re-layouts  14 us (3%)
    pallas_call x1, Pallas kernels, by_planes(): pl.pallas_call(functools.partial(plane_kernel, planes), out_shape=jax.Sha...  403 us
    unnamed x1, local copies, waits for them, and re-layouts  14 us

profile of v3, /device:TPU:19, one launch (start us, length us, event | category | flops | bytes accessed | tf_op | source)
XLA Modules:
  0.0 418.8 jit_solution(13031739563670315305)
XLA Ops:
  0.0 1.4 divide_bitcast_fusion.weights
  1.4 403.4 %shard_map.37 = bf16[2,512,8192]{2,1,0:T(8,128)(2,1)} custom-call(bf16[2,64,128,512]{3,2,1,0:T(8,128)(2,1)} %bitcast.5, s32[64,64]{1,0:T(8,128)} %pat.1, f32[64,128]{1,0:T(8,128)} %divide_bitcast_fusion.weights), custom_call_target="tpu_custom_call" | custom-call | flops 21474836480 | bytes 33554432 | tf_op jit(solution)/shard_map/pallas_call | solution.py:385
  404.8 14.0 %copy.5 = bf16[1,2,512,8192]{3,2,1,0:T(8,128)(2,1)} copy(bf16[1,2,512,8192]{3,2,1,0:T(8,128)(2,1)} %bitcast.4) | data formatting | bytes 33554432
